TPU v7x, 512 devices: a whole 4x8x8 slice. The times are simulated.
512 devices in a mesh: shard: 128 (over z_hi, x, y), tp: 4 (over z_lo, core).
Axes of the slice: x: 4, y: 8, z: 8 (z_hi: 4, z_lo: 2; z = z_hi * 2 + z_lo), core: 2. Of those that a mesh axis runs over, the one named last changes fastest.
Arguments:
- features: bfloat16 [32768, 2048], P('shard', 'tp'), may hold values from -50 to 50, as said below
- item_id: int32 [32768], P('shard'), may hold values from 0 to 262143, as said below
- w_in: bfloat16 [2048, 4096], P('shard', 'tp'), may hold values from -0.125 to 0.125
- bias_in: float32 [4096], P('tp'), may hold values from -3 to 3
- w_out: bfloat16 [1024, 4096], P('shard', 'tp'), may hold values from -16 to 16
- bias_out: float32 [1024], replicated, may hold values from -4 to 4
- item_table: bfloat16 [262144, 1024], P('shard', 'tp'), may hold values from -4 to 4
Outputs:
- new_table: bfloat16 [262144, 1024], P('shard', 'tp')
Inputs may be any that keep to these rules, and one draw needn't show every extreme that they name: `features`: feature rows of order one to sixteen. All ids differ. With owner = item_id // 2048, the 256 items of one index of shard (an aligned block) name one owner at most 4 times, and some owner is named exactly 4 times by every block.
All inputs are finite; a program needn't handle non-finite values.
Results may differ from a plain program's by a relative error of at most 0.0029.
Values may be sent and summed in bfloat16 or wider, within the bound.
No kernel may reach another device: no remote copies, remote signals or barrier semaphores. Data moves between devices by JAX's collectives and lax.ppermute only.
A program may use at most 64 MiB of HBM per device.

v0:
```python
import jax
import jax.numpy as jnp
from jax import lax
from jax.sharding import PartitionSpec as P


def tower(columns, w_in, bias_in, w_out, bias_out):
    gathered = lax.all_gather(columns, "tp", axis=1, tiled=True)
    activation = (
        jnp.dot(
            gathered,
            lax.all_gather(w_in, "shard", axis=0, tiled=True),
            preferred_element_type=jnp.float32,
        )
        + bias_in
    )
    hidden = jax.nn.silu(activation).astype(jnp.bfloat16)
    partial_out = lax.dot_general(
        hidden,
        lax.all_gather(w_out, "shard", axis=0, tiled=True),
        (((1,), (1,)), ((), ())),
        preferred_element_type=jnp.float32,
    )
    width = bias_out.shape[0]
    share_width = width // lax.axis_size("tp")
    offset = lax.axis_index("tp") * share_width
    summed = lax.psum(partial_out, "tp") + bias_out
    scaled = summed * lax.rsqrt(jnp.mean(summed * summed, axis=1, keepdims=True) + 1e-06)
    return lax.dynamic_slice_in_dim(scaled, offset, share_width, 1).astype(jnp.bfloat16)


def local(features, item_id, w_in, bias_in, w_out, bias_out, item_table):
    owners_count = lax.axis_size("shard")
    src_rows = features.shape[0]
    table_rows = item_table.shape[0]
    capacity = 2 * src_rows // owners_count
    owner_index = item_id // table_rows
    local_row = item_id - owner_index * table_rows
    owner_ids = jnp.arange(owners_count, dtype=jnp.int32)
    matches = (owner_index[:, None] == owner_ids[None, :]).astype(jnp.int32)
    within = jnp.sum((jnp.cumsum(matches, axis=0) - 1) * matches, axis=1)
    slot_index = owner_index * capacity + within
    slot_item = jnp.full((owners_count * capacity,), src_rows, jnp.int32)
    slot_item = slot_item.at[slot_index].set(jnp.arange(src_rows, dtype=jnp.int32))
    slot_rows = jnp.take(local_row, slot_item, mode="fill", fill_value=table_rows)
    slot_rows = slot_rows.reshape(owners_count, capacity)
    packed = jnp.take(features, slot_item, axis=0, mode="fill", fill_value=0)
    packed = packed.reshape(owners_count, capacity, features.shape[1])
    arrived, target_rows = (
        lax.all_to_all(packed, "shard", split_axis=0, concat_axis=0, tiled=True),
        lax.all_to_all(slot_rows, "shard", split_axis=0, concat_axis=0, tiled=True),
    )
    arrived_rows = arrived.reshape(owners_count * capacity, features.shape[1])
    embedded = tower(arrived_rows, w_in, bias_in, w_out, bias_out)
    return item_table.at[target_rows.reshape(-1)].set(embedded, mode="drop")


def solution(mesh):
    in_specs = (
        P("shard", "tp"),
        P("shard"),
        P("shard", "tp"),
        P("tp"),
        P("shard", "tp"),
        P(),
        P("shard", "tp"),
    )
    out_specs = P("shard", "tp")
    return jax.shard_map(local, mesh=mesh, in_specs=in_specs, out_specs=out_specs, check_vma=False)
```

profile of v0, /device:TPU:1, one launch (start us, length us, event | category | flops | bytes accessed | tf_op | source)
XLA Modules:
  0.0 400.6 jit_solution(10785810898543927421)
XLA Ops:
  6.5 0.0 copy-start
  6.5 0.0 copy-start.2
  6.5 0.0 all-gather.8.cloned.1.call-start
  6.5 2.3 copy.16
  8.9 0.0 all-gather.8.cloned.1.call-update
  8.9 0.0 all-gather.4.cloned.1.call-start
  8.9 0.0 copy-done.2
  9.0 0.1 copy.10
  9.1 0.2 fusion.5
  9.3 0.1 add_add_fusion
  9.4 0.2 fusion.6
  9.6 1.4 scatter_custom_fusion
  11.0 3.5 gather_fusion
  14.6 0.1 broadcast_in_dim.39
  14.7 0.0 copy-done
  14.7 2.0 gather_fusion.1
  16.7 0.1 gather.12
  16.8 0.0 copy-start.3
  16.8 0.3 broadcast_select_fusion
  17.2 40.8 %all_to_all.11 = bf16[128,4,512]{2,1,0:T(4,128)(2,1)S(1)} all-to-all(bf16[128,4,512]{2,1,0:T(4,128)(2,1)S(1)} %broadcast_select_fusion), channel_id=1, replica_groups=mesh['shard'=128,'tp'=4] {'shard'}, dimensions={0} | all-to-all | bytes 1048576 | tf_op jit(solution)/shard_map/all_to_all | solution.py:50
  57.9 0.9 reshape.102
  58.9 0.0 all-gather.4.cloned.1.call-update
  58.9 0.0 all-gather.6.cloned.1.call-start
  58.9 0.7 all-gather.6.cloned.1.call-update
  59.6 0.0 all-reduce.2.cloned.1.call-start
  59.7 79.7 %all-gather.8.cloned.1.call-done = bf16[1024,1024]{1,0:T(8,128)(2,1)} async-done(((bf16[8,1024]{1,0:T(8,128)(2,1)}), bf16[1024,1024]{1,0:T(8,128)(2,1)}) %all-gather.8.cloned.1.call-update) | async-done | bytes 2097168 | tf_op jit(solution)/shard_map/all_gather | solution.py:20
  139.4 37.1 %all-gather.4.cloned.1.call-done = bf16[512,2048]{1,0:T(8,128)(2,1)} async-done(((bf16[512,512]{1,0:T(8,128)(2,1)}), bf16[512,2048]{1,0:T(8,128)(2,1)}) %all-gather.4.cloned.1.call-update) | async-done | bytes 2097168 | tf_op jit(solution)/shard_map/all_gather | solution.py:8
  176.4 134.7 %all-gather.6.cloned.1.call-done = bf16[2048,1024]{1,0:T(8,128)(2,1)} async-done(((bf16[16,1024]{1,0:T(8,128)(2,1)}), bf16[2048,1024]{1,0:T(8,128)(2,1)}) %all-gather.6.cloned.1.call-update) | async-done | bytes 4194320 | tf_op jit(solution)/shard_map/all_gather | solution.py:12
  311.1 0.0 copy-done.3
  311.1 8.2 %fusion = f32[512,1024]{1,0:T(8,128)} fusion(bf16[1024,1024]{1,0:T(8,128)(2,1)} %all-gather.8.cloned.1.call-done, bf16[512,2048]{1,0:T(8,128)(2,1)} %all-gather.4.cloned.1.call-done, bf16[2048,1024]{1,0:T(8,128)(2,1)} %all-gather.6.cloned.1.call-done, f32[1024]{0:T(1024)S(1)} %copy-done.3), kind=kOutput, calls=%fused_computation.7 | convolution fusion | flops 3224371200 | bytes 10489856 | tf_op jit(solution)/shard_map/dot_general | solution.py:18
  319.4 0.0 copy-start.1
  319.4 0.0 all-reduce.2.cloned.1.call-update
  319.4 0.7 select_n.52
  320.1 11.9 %all-to-all-start = ((s32[128,1,4]{2,1,0:T(1,128)}), s32[128,1,4]{2,1,0:T(1,128)S(1)}, u32[]{:S(2)}, u32[]{:S(2)}) async-start(s32[128,1,4]{2,1,0:T(1,128)} %bitcast.4), calls=%async_computation | async-start | bytes 131072 | tf_op jit(solution)/shard_map/all_to_all | solution.py:51
  332.0 12.4 %all-to-all-done = s32[128,1,4]{2,1,0:T(1,128)S(1)} async-done(((s32[128,1,4]{2,1,0:T(1,128)}), s32[128,1,4]{2,1,0:T(1,128)S(1)}, u32[]{:S(2)}, u32[]{:S(2)}) %all-to-all-start) | async-done | bytes 2080 | tf_op jit(solution)/shard_map/all_to_all | solution.py:51
  344.4 0.5 broadcast.95
  344.9 0.8 reduce.3
  345.7 0.1 reshape.101
  345.9 41.5 %all-reduce.2.cloned.1.call-done = f32[512,1024]{1,0:T(8,128)} async-done(((f32[512,1024]{1,0:T(8,128)}), f32[512,1024]{1,0:T(8,128)}) %all-reduce.2.cloned.1.call-update) | async-done | bytes 2097168 | tf_op jit(solution)/shard_map/psum | solution.py:27
  387.4 0.0 copy-done.1
  387.4 1.9 multiply_reduce_fusion
  389.3 4.8 %scatter_custom_fusion.1 = bf16[2048,256]{1,0:T(8,128)(2,1)} fusion(bf16[2048,256]{1,0:T(8,128)(2,1)} %copy.16, s32[512]{0:T(512)S(1)} %bitcast.15, f32[512,1024]{1,0:T(8,128)S(1)} %get-tuple-element.6, s32[]{:T(128)} %constant.38.clone.1, s32[]{:T(128)S(6)} %select_n.55, f32[512]{0:T(512)S(1)} %add_rsqrt_fusion), kind=kCustom, calls=%fused_computation.11 | custom fusion | flops 262144 | bytes 1575428 | tf_op jit(solution)/shard_map/scatter | solution.py:55
  (12 shorter events, 0.1 us)
Async XLA Ops:
  6.5 8.2 %copy-start = (bf16[256,512]{1,0:T(8,128)(2,1)S(1)}, bf16[256,512]{1,0:T(8,128)(2,1)}, u32[]{:S(2)}) copy-start(bf16[256,512]{1,0:T(8,128)(2,1)} %param.7) | copy-start | bytes 786436
  6.5 2.4 copy-start.2
  6.5 132.8 %all-gather.8.cloned.1.call-start = ((), (), s32[]{:S(2)}) async-start(), calls=%async_computation.4 | async-start | bytes 2113536 | tf_op jit(solution)/shard_map/all_gather | solution.py:20
  8.9 167.6 %all-gather.4.cloned.1.call-start = ((), (), s32[]{:S(2)}) async-start(), calls=%async_computation.2 | async-start | bytes 2621440 | tf_op jit(solution)/shard_map/all_gather | solution.py:8
  16.8 294.3 %copy-start.3 = (f32[1024]{0:T(1024)S(1)}, f32[1024]{0:T(1024)}, u32[]{:S(2)}) copy-start(f32[1024]{0:T(1024)} %param.10) | copy-start | bytes 12292
  58.9 252.3 %all-gather.6.cloned.1.call-start = ((), (), s32[]{:S(2)}) async-start(), calls=%async_computation.3 | async-start | bytes 4227072 | tf_op jit(solution)/shard_map/all_gather | solution.py:12
  59.6 327.7 %all-reduce.2.cloned.1.call-start = ((), (), s32[]{:S(2)}) async-start(), calls=%async_computation.5 | async-start | bytes 4194304 | tf_op jit(solution)/shard_map/psum | solution.py:27
  319.4 68.0 %copy-start.1 = (f32[1024]{0:T(1024)S(1)}, f32[1024]{0:T(1024)}, u32[]{:S(2)}) copy-start(f32[1024]{0:T(1024)} %param.12) | copy-start | bytes 12292
  320.1 24.3 %all-to-all-start = ((s32[128,1,4]{2,1,0:T(1,128)}), s32[128,1,4]{2,1,0:T(1,128)S(1)}, u32[]{:S(2)}, u32[]{:S(2)}) async-start(s32[128,1,4]{2,1,0:T(1,128)} %bitcast.4), calls=%async_computation | async-start | bytes 131072 | tf_op jit(solution)/shard_map/all_to_all | solution.py:51
Sparse Core Ops, SparseCore 0:
  11.8 127.4 all-gather.7
  141.5 34.9 all-gather.3
  180.9 130.1 all-gather.5
  319.5 67.7 all-reduce.1
where the time goes:
time: 401 us
  waiting for transfers between devices  306 us (76%)
  blocking collectives  40.8 us (10%)
  between operations  13.3 us (3%)
  starting transfers between devices  12 us (3%)
  local copies, waits for them, and re-layouts  11.9 us (3%)
  other arithmetic  8.3 us (2%)
  matrix products  8.23 us (2%)
    all_gather x1, waiting for transfers between devices, tower(): lax.all_gather(w_in, 'shard', axis=0, tiled=True)  135 us
    all_gather x1, waiting for transfers between devices, tower(): lax.all_gather(w_out, 'shard', axis=0, tiled=True)  79.7 us
    psum x1, waiting for transfers between devices, tower(): summed = lax.psum(partial_out, 'tp') + bias_out  41.5 us
    all_to_all x1, blocking collectives, local(): lax.all_to_all(packed, 'shard', split_axis=0, concat_axis=0, tiled=True)  40.8 us
    all_gather x1, waiting for transfers between devices, tower(): gathered = lax.all_gather(columns, 'tp', axis=1, tiled=True)  37.1 us
    all_to_all x1, waiting for transfers between devices, local(): lax.all_to_all(slot_rows, 'shard', split_axis=0, concat_axis=0, tiled=True)  12.4 us
    all_to_all x1, starting transfers between devices, local(): lax.all_to_all(slot_rows, 'shard', split_axis=0, concat_axis=0, tiled=True)  11.9 us
    dot_general x1, matrix products, tower(): lax.dot_general(hidden, lax.all_gather(w_out, 'shard', axis=0, tiled=True...  8.23 us
  transfers between devices with their start and end apart: 5, of which 5 were waited for; matrix products, arithmetic and copies ran while one was open for 3% of the time, Pallas kernels for 0%

commit v1 on v0

--- a/solution.py
+++ b/solution.py
@@ -17,7 +17,9 @@
     hidden = jax.nn.silu(activation).astype(jnp.bfloat16)
     partial_out = lax.dot_general(
         hidden,
-        lax.all_gather(w_out, "shard", axis=0, tiled=True),
+        jnp.concatenate(
+            lax.all_to_all(jnp.stack([w_out] * lax.axis_size("shard")), "shard", 0, 0), axis=0
+        ),
         (((1,), (1,)), ((), ())),
         preferred_element_type=jnp.float32,
     )

time: 401 us -> 354 us (0.88)
  waiting for transfers between devices: 306 us -> 200 us
  blocking collectives: 40.8 us -> 100 us
    all_gather x1 -> x0, waiting for transfers between devices: 79.7 us -> none  [tower(): lax.all_gather(w_out, 'shard', axis=0, tiled=True)]
    all_to_all x0 -> x1, blocking collectives: none -> 59.9 us  [tower(): lax.all_to_all(jnp.stack([w_out] * lax.axis_size('shard')), 'shard', 0, 0)]
    all_gather x1, waiting for transfers between devices: 37.1 us -> 11.8 us  [tower(): gathered = lax.all_gather(columns, 'tp', axis=1, tiled=True)]
  transfers between devices with their start and end apart: 5 -> 4, of which waited for: 5 -> 4; matrix products, arithmetic and copies ran while one was open for 3% -> 1% of each run, Pallas kernels for 0% -> 0%
where the time goes in v1:
time: 354 us
  waiting for transfers between devices  200 us (56%)
  blocking collectives  100 us (28%)
  between operations  13.3 us (4%)
  local copies, waits for them, and re-layouts  12.1 us (3%)
  starting transfers between devices  11.8 us (3%)
  other arithmetic  8.3 us (2%)
  matrix products  7.59 us (2%)
    all_gather x1, waiting for transfers between devices, tower(): lax.all_gather(w_in, 'shard', axis=0, tiled=True)  134 us
    all_to_all x1, blocking collectives, tower(): lax.all_to_all(jnp.stack([w_out] * lax.axis_size('shard')), 'shard', 0, 0)  59.9 us
    psum x1, waiting for transfers between devices, tower(): summed = lax.psum(partial_out, 'tp') + bias_out  41.5 us
    all_to_all x1, blocking collectives, local(): lax.all_to_all(packed, 'shard', split_axis=0, concat_axis=0, tiled=True)  40.5 us
    all_to_all x1, waiting for transfers between devices, local(): lax.all_to_all(slot_rows, 'shard', split_axis=0, concat_axis=0, tiled=True)  12.6 us
    all_gather x1, waiting for transfers between devices, tower(): gathered = lax.all_gather(columns, 'tp', axis=1, tiled=True)  11.8 us
    all_to_all x1, starting transfers between devices, local(): lax.all_to_all(slot_rows, 'shard', split_axis=0, concat_axis=0, tiled=True)  11.7 us
    dot_general x1, matrix products, tower(): lax.dot_general(hidden, jnp.concatenate(lax.all_to_all(jnp.stack([w_out]...  7.59 us
  transfers between devices with their start and end apart: 4, of which 4 were waited for; matrix products, arithmetic and copies ran while one was open for 1% of the time, Pallas kernels for 0%

profile of v1, /device:TPU:1, one launch (start us, length us, event | category | flops | bytes accessed | tf_op | source)
XLA Modules:
  0.0 353.9 jit_solution(6272901891209566429)
XLA Ops:
  6.5 0.0 copy-start
  6.5 0.0 copy-start.3
  6.5 0.0 all-gather.3.cloned.1.call-start
  6.5 2.3 copy.16
  8.9 0.0 copy-done.3
  8.9 0.1 copy.10
  9.0 0.2 fusion.6
  9.2 0.1 add_add_fusion
  9.3 0.2 fusion.7
  9.5 1.4 scatter_custom_fusion
  11.0 3.5 gather_fusion
  14.5 0.1 broadcast_in_dim.39
  14.6 0.0 copy-done
  14.6 2.0 gather_fusion.1
  16.6 0.1 gather.12
  16.7 0.0 copy-start.1
  16.7 0.3 broadcast_select_fusion
  17.1 40.5 %all_to_all.16 = bf16[128,4,512]{2,1,0:T(4,128)(2,1)S(1)} all-to-all(bf16[128,4,512]{2,1,0:T(4,128)(2,1)S(1)} %broadcast_select_fusion), channel_id=1, replica_groups=mesh['shard'=128,'tp'=4] {'shard'}, dimensions={0} | all-to-all | bytes 1048576 | tf_op jit(solution)/shard_map/all_to_all | solution.py:52
  57.6 0.9 reshape.107
  58.5 0.0 all-gather.3.cloned.1.call-update
  58.5 0.0 all-gather.5.cloned.1.call-start
  58.6 0.7 all-gather.5.cloned.1.call-update
  59.3 0.0 all-reduce.2.cloned.1.call-start
  59.3 0.0 copy-done.1
  59.3 0.2 stack.2
  59.6 0.0 copy-start.4
  59.6 59.9 %all_to_all.17 = bf16[128,8,1024]{2,1,0:T(8,128)(2,1)S(1)} all-to-all(bf16[128,8,1024]{2,1,0:T(8,128)(2,1)S(1)} %stack.2), channel_id=1, replica_groups=mesh['shard'=128,'tp'=4] {'shard'}, dimensions={0} | all-to-all | bytes 4194304 | tf_op jit(solution)/shard_map/all_to_all | solution.py:21
  119.5 11.8 %all-gather.3.cloned.1.call-done = bf16[512,2048]{1,0:T(8,128)(2,1)} async-done(((bf16[512,512]{1,0:T(8,128)(2,1)}), bf16[512,2048]{1,0:T(8,128)(2,1)}) %all-gather.3.cloned.1.call-update) | async-done | bytes 2097168 | tf_op jit(solution)/shard_map/all_gather | solution.py:8
  131.4 133.7 %all-gather.5.cloned.1.call-done = bf16[2048,1024]{1,0:T(8,128)(2,1)} async-done(((bf16[16,1024]{1,0:T(8,128)(2,1)}), bf16[2048,1024]{1,0:T(8,128)(2,1)}) %all-gather.5.cloned.1.call-update) | async-done | bytes 4194320 | tf_op jit(solution)/shard_map/all_gather | solution.py:12
  265.1 0.0 copy-done.4
  265.1 7.6 %fusion = f32[512,1024]{1,0:T(8,128)} fusion(bf16[128,8,1024]{2,1,0:T(8,128)(2,1)S(1)} %all_to_all.17, bf16[512,2048]{1,0:T(8,128)(2,1)} %all-gather.3.cloned.1.call-done, bf16[2048,1024]{1,0:T(8,128)(2,1)} %all-gather.5.cloned.1.call-done, f32[1024]{0:T(1024)S(1)} %copy-done.4), kind=kOutput, calls=%fused_computation.4 | convolution fusion | flops 3224371200 | bytes 10489856 | tf_op jit(solution)/shard_map/dot_general | solution.py:18
  272.7 0.0 copy-start.2
  272.7 0.0 all-reduce.2.cloned.1.call-update
  272.7 0.7 select_n.52
  273.5 11.7 %all-to-all-start = ((s32[128,1,4]{2,1,0:T(1,128)}), s32[128,1,4]{2,1,0:T(1,128)S(1)}, u32[]{:S(2)}, u32[]{:S(2)}) async-start(s32[128,1,4]{2,1,0:T(1,128)} %bitcast.4), calls=%async_computation | async-start | bytes 131072 | tf_op jit(solution)/shard_map/all_to_all | solution.py:53
  285.2 12.6 %all-to-all-done = s32[128,1,4]{2,1,0:T(1,128)S(1)} async-done(((s32[128,1,4]{2,1,0:T(1,128)}), s32[128,1,4]{2,1,0:T(1,128)S(1)}, u32[]{:S(2)}, u32[]{:S(2)}) %all-to-all-start) | async-done | bytes 2080 | tf_op jit(solution)/shard_map/all_to_all | solution.py:53
  297.8 0.5 broadcast.97
  298.3 0.8 reduce.3
  299.1 0.1 reshape.106
  299.2 41.5 %all-reduce.2.cloned.1.call-done = f32[512,1024]{1,0:T(8,128)} async-done(((f32[512,1024]{1,0:T(8,128)}), f32[512,1024]{1,0:T(8,128)}) %all-reduce.2.cloned.1.call-update) | async-done | bytes 2097168 | tf_op jit(solution)/shard_map/psum | solution.py:29
  340.7 0.0 copy-done.2
  340.7 1.9 multiply_reduce_fusion
  342.6 4.8 %scatter_custom_fusion.1 = bf16[2048,256]{1,0:T(8,128)(2,1)} fusion(bf16[2048,256]{1,0:T(8,128)(2,1)} %copy.16, s32[512]{0:T(512)S(1)} %bitcast.17, f32[512,1024]{1,0:T(8,128)S(1)} %get-tuple-element.6, s32[]{:T(128)} %constant.38.clone.1, s32[]{:T(128)S(6)} %select_n.55, f32[512]{0:T(512)S(1)} %add_rsqrt_fusion), kind=kCustom, calls=%fused_computation.12 | custom fusion | flops 262144 | bytes 1575428 | tf_op jit(solution)/shard_map/scatter | solution.py:57
  (12 shorter events, 0.1 us)
Async XLA Ops:
  6.5 8.1 %copy-start = (bf16[256,512]{1,0:T(8,128)(2,1)S(1)}, bf16[256,512]{1,0:T(8,128)(2,1)}, u32[]{:S(2)}) copy-start(bf16[256,512]{1,0:T(8,128)(2,1)} %param.7) | copy-start | bytes 786436
  6.5 2.3 copy-start.3
  6.5 124.8 %all-gather.3.cloned.1.call-start = ((), (), s32[]{:S(2)}) async-start(), calls=%async_computation.3 | async-start | bytes 2621440 | tf_op jit(solution)/shard_map/all_gather | solution.py:8
  16.7 42.6 %copy-start.1 = (bf16[8,1024]{1,0:T(8,128)(2,1)S(1)}, bf16[8,1024]{1,0:T(8,128)(2,1)}, u32[]{:S(2)}) copy-start(bf16[8,1024]{1,0:T(8,128)(2,1)} %param.11) | copy-start | bytes 49156
  58.5 206.6 %all-gather.5.cloned.1.call-start = ((), (), s32[]{:S(2)}) async-start(), calls=%async_computation.4 | async-start | bytes 4227072 | tf_op jit(solution)/shard_map/all_gather | solution.py:12
  59.3 281.4 %all-reduce.2.cloned.1.call-start = ((), (), s32[]{:S(2)}) async-start(), calls=%async_computation.5 | async-start | bytes 4194304 | tf_op jit(solution)/shard_map/psum | solution.py:29
  59.6 205.5 %copy-start.4 = (f32[1024]{0:T(1024)S(1)}, f32[1024]{0:T(1024)}, u32[]{:S(2)}) copy-start(f32[1024]{0:T(1024)} %param.10) | copy-start | bytes 12292
  272.7 68.0 %copy-start.2 = (f32[1024]{0:T(1024)S(1)}, f32[1024]{0:T(1024)}, u32[]{:S(2)}) copy-start(f32[1024]{0:T(1024)} %param.12) | copy-start | bytes 12292
  273.5 24.3 %all-to-all-start = ((s32[128,1,4]{2,1,0:T(1,128)}), s32[128,1,4]{2,1,0:T(1,128)S(1)}, u32[]{:S(2)}, u32[]{:S(2)}) async-start(s32[128,1,4]{2,1,0:T(1,128)} %bitcast.4), calls=%async_computation | async-start | bytes 131072 | tf_op jit(solution)/shard_map/all_to_all | solution.py:53
Sparse Core Ops, SparseCore 0:
  58.6 72.6 all-gather.2
  135.9 129.2 all-gather.4
  272.9 67.7 all-reduce.1
